TPU v7x, 256 devices: a whole 4x4x8 slice. The times are simulated.
256 devices in a mesh: row: 8 (over z), col: 32 (over x, y, core).
Axes of the slice: x: 4, y: 4, z: 8, core: 2. Of those that a mesh axis runs over, the one named last changes fastest.
Arguments:
- trailing: float32 [32768, 12288], P('row', 'col'), may hold values from -6 to 6
- leaf_vectors: float32 [32768, 256], P(('row', 'col')), may hold values from -1 to 1, as said below
- leaf_factor: float32 [2048, 256], P(('row', 'col')), may hold values from -1 to 2, as said below
- tree_vectors: float32 [2048, 256], P(('row', 'col')), may hold values from -1 to 1, as said below
- tree_factor: float32 [2048, 256], P(('row', 'col')), may hold values from -1 to 2, as said below
Outputs:
- updated: float32 [32768, 12288], P('row', 'col')
Inputs may be any that keep to these rules, and one draw needn't show every extreme that they name: `leaf_vectors`: in each row block of 4096 rows, row r < 256 of the block holds 1 in column r and 0 in every column after r. `leaf_factor`: each 256 x 256 block is upper triangular with its diagonal between 1 and 2. `tree_vectors`: each 256 x 256 block is upper triangular. `tree_factor`: each 256 x 256 block is upper triangular with its diagonal between 1 and 2.
All inputs are finite; a program needn't handle non-finite values.
Results may differ from a plain program's by a relative error of at most 0.0002.
Values sent between devices are 32-bit elements; how exact they have to be, the bound alone decides.
A program may use at most 128 MiB of HBM per device.

v0:
```python
import jax
import jax.numpy as jnp
from jax import lax
from jax.sharding import PartitionSpec as P

highest = lax.Precision.HIGHEST
contract_rows = (((0,), (0,)), ((), ()))


def left_product(first, second):
    return lax.dot_general(
        first, second, contract_rows, precision=highest, preferred_element_type=jnp.float32
    )


def plain_product(first, second):
    return jnp.dot(first, second, precision=highest, preferred_element_type=jnp.float32)


def shards(trailing, leaf_vectors, leaf_factor, tree_vectors, tree_factor):
    panel_width = leaf_factor.shape[1]
    panel, block_factor, own_vectors, own_factor = (
        lax.all_gather(leaf_vectors, "col", axis=0, tiled=True),
        lax.all_gather(leaf_factor, "col", axis=0, tiled=True),
        lax.all_gather(tree_vectors, "col", axis=0, tiled=True),
        lax.all_gather(tree_factor, "col", axis=0, tiled=True),
    )
    weights = left_product(block_factor, left_product(panel, trailing))
    updated = trailing - plain_product(panel, weights)
    upper_rows = updated[:panel_width]
    lower_rows = updated[panel_width:]
    sections = lax.axis_size("row").bit_length() - 1
    blocks_count = lax.axis_size("row")
    position = lax.axis_index("row")
    all_tops, all_vectors, all_factors = (
        lax.all_gather(upper_rows[None], "row", axis=0, tiled=True),
        lax.all_gather(own_vectors[None], "row", axis=0, tiled=True),
        lax.all_gather(own_factor[None], "row", axis=0, tiled=True),
    )
    columns = upper_rows.shape[1]
    for level_bit in range(sections):
        stride = 1 << level_bit
        groups = blocks_count // (2 * stride)
        grouped = all_tops.reshape(groups, 2 * stride, panel_width, columns)
        leaders = grouped[:, 0]
        partners = grouped[:, stride]
        vectors = all_vectors.reshape(groups, 2 * stride, panel_width, panel_width)[:, stride]
        factors = all_factors.reshape(groups, 2 * stride, panel_width, panel_width)[:, stride]
        inner = leaders + jnp.einsum(
            "gji,gjc->gic", vectors, partners, precision=highest, preferred_element_type=jnp.float32
        )
        tree_weights = jnp.einsum(
            "gji,gjc->gic", factors, inner, precision=highest, preferred_element_type=jnp.float32
        )
        moved = jnp.einsum(
            "gij,gjc->gic",
            vectors,
            tree_weights,
            precision=highest,
            preferred_element_type=jnp.float32,
        )
        grouped = grouped.at[:, 0].set(leaders - tree_weights).at[:, stride].set(partners - moved)
        all_tops = grouped.reshape(blocks_count, panel_width, columns)
    final_top = lax.dynamic_index_in_dim(all_tops, position, 0, keepdims=False)
    return jnp.concatenate([final_top, lower_rows], 0)


def solution(mesh):
    placed = (
        P("row", "col"),
        P(("row", "col"), None),
        P(("row", "col"), None),
        P(("row", "col"), None),
        P(("row", "col"), None),
    )
    return jax.shard_map(
        shards, mesh=mesh, in_specs=placed, out_specs=P("row", "col"), check_vma=False
    )
```

profile of v0, /device:TPU:1, one launch (start us, length us, event | category | flops | bytes accessed | tf_op | source)
XLA Modules:
  0.0 242.6 jit_solution(14304152911866550138)
XLA Ops:
  7.3 6.6 %copy.16 = f32[4096,384]{0,1:T(8,128)} copy(f32[4096,384]{1,0:T(8,128)} %param.17) | data formatting | bytes 12582912 | tf_op args[0]
  13.9 26.4 %all_gather.22 = f32[256,256]{1,0:T(8,128)S(1)} all-gather(f32[8,256]{1,0:T(8,128)S(1)} %copy-done.6), channel_id=1, replica_groups=mesh['row'=8,'col'=32] {'col'}, dimensions={0}, use_global_device_ids=true | all-gather | bytes 270336 | tf_op jit(solution)/shard_map/all_gather | solution.py:24
  40.3 25.0 %all-gather.8.cloned.1.call-done = f32[4096,256]{1,0:T(8,128)} async-done(((f32[128,256]{1,0:T(8,128)}), f32[4096,256]{1,0:T(8,128)}) %all-gather.8.cloned.1.call-update) | async-done | bytes 4194320 | tf_op jit(solution)/shard_map/all_gather | solution.py:23
  65.3 9.7 %fusion.15 = f32[256,384]{1,0:T(8,128)S(1)} fusion(f32[4096,256]{1,0:T(8,128)} %all-gather.8.cloned.1.call-done, f32[4096,384]{1,0:T(8,128)} %param.17), kind=kOutput, calls=%fused_computation.41 | convolution fusion | flops 4831838208 | bytes 10878976 | tf_op jit(solution)/shard_map/dot_general | solution.py:11
  75.8 6.0 %bitcast_subtract_fusion = f32[4096,384]{0,1:T(8,128)S(1)} fusion(f32[4096,384]{0,1:T(8,128)S(1)} %copy-done.1, f32[384,256]{1,0:T(8,128)S(1)} %fusion.16, f32[4096,256]{1,0:T(8,128)S(1)} %copy-done.3), kind=kOutput, calls=%fused_computation.1 | convolution fusion | flops 4833411072 | bytes 17170432 | tf_op jit(solution)/shard_map/dot_general | solution.py:17
  81.9 2.7 %copy-done = f32[4096,384]{0,1:T(8,128)} copy-done((f32[4096,384]{0,1:T(8,128)}, f32[4096,384]{0,1:T(8,128)S(1)}, u32[]{:S(2)}) %copy-start) | copy-done | bytes 6291480
  85.4 26.5 %all_gather.24 = f32[256,256]{1,0:T(8,128)} all-gather(f32[8,256]{1,0:T(8,128)S(1)} %copy-done.7), channel_id=1, replica_groups=mesh['row'=8,'col'=32] {'col'}, dimensions={0}, use_global_device_ids=true | all-gather | bytes 270336 | tf_op jit(solution)/shard_map/all_gather | solution.py:25
  112.0 24.7 %all_gather.26 = f32[256,256]{1,0:T(8,128)} all-gather(f32[8,256]{1,0:T(8,128)S(1)} %copy-done.8), channel_id=1, replica_groups=mesh['row'=8,'col'=32] {'col'}, dimensions={0}, use_global_device_ids=true | all-gather | bytes 270336 | tf_op jit(solution)/shard_map/all_gather | solution.py:26
  136.8 5.6 %slice.219 = f32[3840,384]{0,1:T(8,128)} slice(f32[4096,384]{0,1:T(8,128)} %copy-done), slice={[256:4096], [0:384]} | slice | bytes 11796480 | tf_op jit(solution)/shard_map/slice | solution.py:31
  142.4 4.2 %reshape.270 = f32[4,2,256,384]{2,1,0,3:T(2,128)S(1)} reshape(f32[2048,384]{0,1:T(8,128)} %all-gather.10.cloned.1.call-done) | data formatting | bytes 6291456 | tf_op jit(solution)/shard_map/reshape | solution.py:44
  146.6 3.4 %copy.21 = f32[4,2,256,384]{3,2,1,0:T(8,128)} copy(f32[4,2,256,384]{2,1,0,3:T(2,128)S(1)} %reshape.270) | data formatting | bytes 6291456 | tf_op jit(solution)/shard_map/reshape | solution.py:44
  150.0 4.1 %fusion.14 = (f32[4,1,256,384]{2,1,0,3:T(1,128)}, f32[4,1,256,384]{2,1,0,3:T(1,128)}) fusion(f32[4,2,256,384]{2,1,0,3:T(2,128)S(1)} %reshape.270), kind=kLoop, calls=%fused_computation.40 | loop fusion | bytes 6291456 | tf_op jit(solution)/shard_map/slice | solution.py:45
  154.1 4.9 %copy.36 = f32[4,1,256,384]{3,2,0,1:T(8,128)} copy(f32[4,1,256,384]{2,1,0,3:T(1,128)} %get-tuple-element.77) | data formatting | bytes 3145728
  159.0 5.1 %copy.37 = f32[4,1,256,384]{3,2,0,1:T(8,128)} copy(f32[4,1,256,384]{2,1,0,3:T(1,128)} %get-tuple-element.78) | data formatting | bytes 3145728
  164.0 3.4 %all-gather.12.cloned.1.call-done = f32[2048,256]{1,0:T(8,128)} async-done(((f32[256,256]{1,0:T(8,128)}), f32[2048,256]{1,0:T(8,128)}) %all-gather.12.cloned.1.call-update) | async-done | bytes 2097168 | tf_op jit(solution)/shard_map/all_gather | solution.py:37
  167.4 4.8 %fusion.1 = f32[4,384,256]{1,2,0:T(8,128)} fusion(f32[4,1,256,384]{3,2,0,1:T(8,128)} %copy.37, f32[4,2,256,256]{3,2,1,0:T(8,128)} %bitcast.171), kind=kOutput, calls=%fused_computation.8 | convolution fusion | flops 1207959552 | bytes 4194304 | tf_op jit(solution)/shard_map/gji,gjc->gic/dot_general | solution.py:49
  172.2 36.6 %all-gather.14.cloned.1.call-done = f32[2048,256]{1,0:T(8,128)} async-done(((f32[256,256]{1,0:T(8,128)}), f32[2048,256]{1,0:T(8,128)}) %all-gather.14.cloned.1.call-update) | async-done | bytes 2097168 | tf_op jit(solution)/shard_map/all_gather | solution.py:38
  208.7 4.8 %bitcast_dynamic-update-slice_fusion.1 = (f32[4,2,256,384]{3,2,1,0:T(8,128)S(1)}, f32[4,384,256]{1,2,0:T(8,128)S(1)}) fusion(f32[4,2,256,384]{3,2,1,0:T(8,128)S(1)} %copy-done.2, f32[4,1,256,384]{3,2,0,1:T(8,128)} %copy.36, f32[4,2,256,256]{3,2,1,0:T(8,128)} %bitcast.177, f32[4,384,256]{1,2,0:T(8,128)} %fusion.1), kind=kOutput, calls=%fused_computation.3 | convolution fusion | flops 1208745984 | bytes 8912896 | tf_op jit(solution)/shard_map/gji,gjc->gic/dot_general | solution.py:52
  213.6 2.0 bitcast_dynamic-update-slice_fusion
  215.9 1.1 fusion.4
  216.9 2.1 bitcast_dynamic-update-slice_fusion.2
  221.0 1.6 bitcast_dynamic-update-slice_fusion.3
  223.5 6.1 %pad_maximum_fusion = f32[4096,384]{0,1:T(8,128)} fusion(f32[3840,384]{0,1:T(8,128)} %slice.219, f32[256,384]{0,1:T(8,128)S(1)} %bitcast.180), kind=kLoop, calls=%fused_computation | loop fusion | flops 1572864 | bytes 12582912 | tf_op jit(solution)/shard_map/concatenate | solution.py:65
  229.5 6.6 %copy.33 = f32[4096,384]{1,0:T(8,128)} copy(f32[4096,384]{0,1:T(8,128)} %pad_maximum_fusion) | data formatting | bytes 12582912 | tf_op jit(solution)/shard_map/concatenate | solution.py:65
  (36 shorter events, 5.5 us)
Async XLA Ops:
  6.5 58.7 %all-gather.8.cloned.1.call-start = ((), (), s32[]{:S(2)}) async-start(), calls=%async_computation | async-start | bytes 4325376 | tf_op jit(solution)/shard_map/all_gather | solution.py:23
  7.3 6.6 %copy-start.6 = (f32[8,256]{1,0:T(8,128)S(1)}, f32[8,256]{1,0:T(8,128)}, u32[]{:S(2)}) copy-start(f32[8,256]{1,0:T(8,128)} %param.19) | copy-start | bytes 24580
  7.3 135.1 %all-gather.10.cloned.1.call-start = ((), (), s32[]{:S(2)}) async-start(), calls=%async_computation.1 | async-start | bytes 3538944 | tf_op jit(solution)/shard_map/all_gather | solution.py:36
  65.2 10.5 %copy-start.1 = (f32[4096,384]{0,1:T(8,128)S(1)}, f32[4096,384]{0,1:T(8,128)}, u32[]{:S(2)}) copy-start(f32[4096,384]{0,1:T(8,128)} %copy.16) | copy-start | bytes 18874372
  65.3 10.6 %copy-start.3 = (f32[4096,256]{1,0:T(8,128)S(1)}, f32[4096,256]{1,0:T(8,128)}, u32[]{:S(2)}) copy-start(f32[4096,256]{1,0:T(8,128)} %all-gather.8.cloned.1.call-done) | copy-start | bytes 12582916
  75.8 9.6 %copy-start.7 = (f32[8,256]{1,0:T(8,128)S(1)}, f32[8,256]{1,0:T(8,128)}, u32[]{:S(2)}) copy-start(f32[8,256]{1,0:T(8,128)} %param.20) | copy-start | bytes 24580
  75.8 36.2 %copy-start.8 = (f32[8,256]{1,0:T(8,128)S(1)}, f32[8,256]{1,0:T(8,128)}, u32[]{:S(2)}) copy-start(f32[8,256]{1,0:T(8,128)} %param.21) | copy-start | bytes 24580
  81.9 2.7 %copy-start = (f32[4096,384]{0,1:T(8,128)}, f32[4096,384]{0,1:T(8,128)S(1)}, u32[]{:S(2)}) copy-start(f32[4096,384]{0,1:T(8,128)S(1)} %bitcast_subtract_fusion) | copy-start | bytes 18874372
  85.4 82.0 %all-gather.12.cloned.1.call-start = ((), (), s32[]{:S(2)}) async-start(), calls=%async_computation.2 | async-start | bytes 2359296 | tf_op jit(solution)/shard_map/all_gather | solution.py:37
  111.9 96.8 %all-gather.14.cloned.1.call-start = ((), (), s32[]{:S(2)}) async-start(), calls=%async_computation.3 | async-start | bytes 2359296 | tf_op jit(solution)/shard_map/all_gather | solution.py:38
  159.0 49.8 %copy-start.2 = (f32[4,2,256,384]{3,2,1,0:T(8,128)S(1)}, f32[4,2,256,384]{3,2,1,0:T(8,128)}, u32[]{:S(2)}) copy-start(f32[4,2,256,384]{3,2,1,0:T(8,128)} %copy.21) | copy-start | bytes 9437188
  208.7 4.8 %copy-start.4 = (f32[4,1,256,384]{3,2,0,1:T(8,128)S(1)}, f32[4,1,256,384]{3,2,0,1:T(8,128)}, u32[]{:S(2)}) copy-start(f32[4,1,256,384]{3,2,0,1:T(8,128)} %copy.37) | copy-start | bytes 4718596
  208.7 4.8 %copy-start.5 = (f32[2048,256]{1,0:T(8,128)S(1)}, f32[2048,256]{1,0:T(8,128)}, u32[]{:S(2)}) copy-start(f32[2048,256]{1,0:T(8,128)} %all-gather.12.cloned.1.call-done) | copy-start | bytes 6291460
Sparse Core Ops, SparseCore 0:
  9.9 55.2 all-gather.7
  85.5 43.7 all-gather.9
  131.1 36.2 all-gather.11
  169.0 39.6 all-gather.13
where the time goes:
time: 246 us; the launch traced here: 243 us
  blocking collectives  77.6 us (32%)
  waiting for transfers between devices  65.7 us (27%)
  local copies, waits for them, and re-layouts  44.6 us (18%)
  matrix products  35.2 us (14%)
  between operations  13.4 us (5%)
  other arithmetic  6.06 us (2%)
    all_gather x1, waiting for transfers between devices, shards(): lax.all_gather(own_factor[None], 'row', axis=0, tiled=True)  36.6 us
    all_gather x1, blocking collectives, shards(): lax.all_gather(tree_vectors, 'col', axis=0, tiled=True)  26.5 us
    all_gather x1, blocking collectives, shards(): lax.all_gather(leaf_factor, 'col', axis=0, tiled=True)  26.4 us
    all_gather x1, waiting for transfers between devices, shards(): lax.all_gather(leaf_vectors, 'col', axis=0, tiled=True)  25 us
    all_gather x1, blocking collectives, shards(): lax.all_gather(tree_factor, 'col', axis=0, tiled=True)  24.7 us
    unnamed x23, local copies, waits for them, and re-layouts  19.7 us
    dot_general x2, matrix products, left_product(): lax.dot_general(first, second, contract_rows, precision=highest, preferre...  10.5 us
    dot_general x3, matrix products, shards(): jnp.einsum('gji,gjc->gic', factors, inner, precision=highest, preferred_e...  8.5 us
  transfers between devices with their start and end apart: 4, of which 3 were waited for; matrix products, arithmetic and copies ran while one was open for 16% of the time, Pallas kernels for 0%

commit v1 on v0

v1 whole, which is shorter than its diff:
```python
import jax
import jax.numpy as jnp
from jax import lax
from jax.experimental import pallas as pl
from jax.experimental.pallas import tpu as pltpu
from jax.sharding import PartitionSpec as P

MESH = pl.DeviceIdType.MESH
HIGH = lax.Precision.HIGH
F32 = jnp.float32

PANEL = 256
ROWS = 4096
COLS = 384
CHUNK = 128
CHUNKS = COLS // CHUNK
SIDE = 4
CHIPS = 16
DEVS = 32

BLOCK = 168
OWN_U, OWN_F = 64, 72
SECOND = 80
S_ROW = 144
FOREIGN = 152
STREAMS = ((0, 80, 40, 0), (SECOND, 72, 40, 1), (FOREIGN, 16, 8, 1))

CLASSES = (
    ((1, 0), (3, 0), (0, 1), (0, 3)),
    ((2, 0), (0, 2)),
    ((1, 1), (1, 3), (3, 1), (3, 3)),
    ((1, 2), (3, 2), (2, 1), (2, 3)),
    ((2, 2),),
)


def pick(index, values):
    result = jnp.int32(values[-1])
    for k in range(len(values) - 2, -1, -1):
        result = jnp.where(index == k, jnp.int32(values[k]), result)
    return result


def dot(a, b):
    return jnp.dot(a, b, precision=HIGH, preferred_element_type=F32)


def dot_t(a, b):
    return lax.dot_general(a, b, (((0,), (0,)), ((), ())), precision=HIGH, preferred_element_type=F32)


def kernel(
    c_hbm, v_hbm, s_hbm, u_hbm, f_hbm, out_hbm,
    buf, cbuf, zacc, wacc, xown, pair, leads, xfin, fac_u, fac_ut, fac_ft,
    load_sem, c_sem, send_sem, recv_sem, half_sem, sib_sem, sib2_sem, uf_send, uf_recv,
    a_send, a_recv, b_send, b_recv, l_send, l_recv, out_sem, top_sem,
):
    z = lax.axis_index("row")
    col = lax.axis_index("col")
    core = lax.rem(col, 2)
    chip = lax.div(col, 2)
    x = lax.div(chip, SIDE)
    y = lax.rem(chip, SIDE)
    role = lax.rem(z, 4)
    group = lax.div(z, 4)
    sibling = col + 1 - 2 * core

    def chip_at(dx, dy):
        return lax.rem(x + dx, SIDE) * SIDE + lax.rem(y + dy, SIDE)

    def neighbour(axis, step):
        return chip_at(step, 0) * 2 + core if axis == 0 else chip_at(0, step) * 2 + core

    loads = [
        pltpu.make_async_copy(v_hbm.at[pl.ds(0, 64)], buf.at[col, pl.ds(0, 64)], load_sem.at[0]),
        pltpu.make_async_copy(v_hbm.at[pl.ds(64, 64)], buf.at[col, pl.ds(SECOND, 64)], load_sem.at[1]),
        pltpu.make_async_copy(s_hbm, buf.at[col, pl.ds(S_ROW, 8)], load_sem.at[2]),
        pltpu.make_async_copy(u_hbm, buf.at[col, pl.ds(OWN_U, 8)], load_sem.at[3]),
        pltpu.make_async_copy(f_hbm, buf.at[col, pl.ds(OWN_F, 8)], load_sem.at[4]),
    ]
    for load in loads:
        load.start()
    load_c = pltpu.make_async_copy(c_hbm, cbuf, c_sem)
    load_c.start()

    barrier = pltpu.get_barrier_semaphore()
    for axis in (0, 1):
        for step in (1, 3):
            pl.semaphore_signal(barrier, inc=1, device_id=(z, neighbour(axis, step)), device_id_type=MESH)
    pl.semaphore_signal(barrier, inc=1, device_id=(z, sibling), device_id_type=MESH)
    for step in range(1, 8):
        pl.semaphore_signal(barrier, inc=1, device_id=(lax.rem(z + step, 8), col), device_id_type=MESH)
    pl.semaphore_wait(barrier, 12)
    for load in loads:
        load.wait()

    uf_to = pick(z, (3, 4, 1, 2, 0, 7, 5, 6))
    uf_copy = pltpu.make_async_remote_copy(
        src_ref=buf.at[col, pl.ds(OWN_U, 16)], dst_ref=buf.at[col, pl.ds(FOREIGN, 16)],
        send_sem=uf_send, recv_sem=uf_recv, device_id=(uf_to, col), device_id_type=MESH,
    )
    uf_copy.start()

    def send(block, start, rows, to, sem):
        pltpu.make_async_remote_copy(
            src_ref=buf.at[block, pl.ds(start, rows)], dst_ref=buf.at[block, pl.ds(start, rows)],
            send_sem=send_sem, recv_sem=sem, device_id=(z, to), device_id_type=MESH,
        ).start()

    def arrived(block, start, rows, sem):
        pltpu.make_async_copy(buf.at[block, pl.ds(start, rows)], buf.at[block, pl.ds(start, rows)], sem).wait()

    def offset_index(axis, i, j):
        i, j = i % SIDE, j % SIDE
        return (i * SIDE + j) if axis == 0 else (j * SIDE + i)

    def handle(h, dx, dy):
        start, rows, front, axis = STREAMS[h]
        i, j = (dx, dy) if axis == 0 else (dy, dx)
        block = chip_at(dx, dy) * 2 + core
        here = offset_index(axis, i, j)
        other = 1 - axis
        if (i, j) != (0, 0):
            if j == 2 or (j == 0 and i == 2):
                arrived(block, start, front, recv_sem.at[h, here])
                arrived(block, start + front, rows - front, half_sem.at[h, here])
            else:
                arrived(block, start, rows, recv_sem.at[h, here])
        if j == 0:
            if i == 0:
                send(block, start, rows, neighbour(axis, 1), recv_sem.at[h, offset_index(axis, 3, 0)])
                send(block, start, rows, neighbour(axis, 3), recv_sem.at[h, offset_index(axis, 1, 0)])
            elif i == 3:
                send(block, start, front, neighbour(axis, 1), recv_sem.at[h, offset_index(axis, 2, 0)])
            elif i == 1:
                send(block, start + front, rows - front, neighbour(axis, 3), half_sem.at[h, offset_index(axis, 2, 0)])
            send(block, start, rows, neighbour(other, 1), recv_sem.at[h, offset_index(axis, i, 3)])
            send(block, start, rows, neighbour(other, 3), recv_sem.at[h, offset_index(axis, i, 1)])
        elif j == 3:
            send(block, start, front, neighbour(other, 1), recv_sem.at[h, offset_index(axis, i, 2)])
        elif j == 1:
            send(block, start + front, rows - front, neighbour(other, 3), half_sem.at[h, offset_index(axis, i, 2)])
        send(block, start, rows, sibling, sib2_sem if h == 2 else sib_sem.at[h, here])

    def vectors(q):
        parts = []
        for k in (0, 1):
            parts += [buf[2 * q + k, pl.ds(0, 64), :], buf[2 * q + k, pl.ds(SECOND, 64), :]]
        return jnp.concatenate(parts, axis=0)

    def project(chips):
        @pl.loop(0, len(chips))
        def _(t):
            dx = pick(t, [c[0] for c in chips])
            dy = pick(t, [c[1] for c in chips])
            q = chip_at(dx, dy)
            block = 2 * q + 1 - core
            for h in (0, 1):
                arrived(block, STREAMS[h][0], STREAMS[h][1], sib_sem.at[h, dx * SIDE + dy])
            rows = pl.ds(pl.multiple_of(q * 256, 256), 256)
            zacc[...] += dot_t(vectors(q), cbuf[rows, :])

    handle(0, 0, 0)
    handle(1, 0, 0)
    zacc[...] = jnp.zeros_like(zacc)
    load_c.wait()
    uf_copy.wait()
    ready = ((0, 0),)
    for n, chips in enumerate(CLASSES):
        for h in (0, 1):
            for dx, dy in chips:
                handle(h, dx, dy)
        for dx, dy in (CLASSES[n - 1] if n else ((0, 0),)):
            handle(2, dx, dy)
        if n:
            project(ready + CLASSES[0] if n == 1 else CLASSES[n - 1])
    handle(2, 2, 2)
    project(CLASSES[-1])

    factor = buf[:, pl.ds(S_ROW, 8), :].reshape(PANEL, PANEL)
    wacc[...] = dot_t(factor, zacc[...])
    top = cbuf[pl.ds(0, PANEL), :] - dot(vectors(jnp.int32(0)), wacc[...])
    for c in range(CHUNKS):
        xown[c] = top[:, c * CHUNK : (c + 1) * CHUNK]

    def a_copy(c):
        to = jnp.where(role == 3, z - 1, z + 1)
        return pltpu.make_async_remote_copy(
            src_ref=xown.at[c], dst_ref=pair.at[0, c], send_sem=a_send.at[c], recv_sem=a_recv.at[c],
            device_id=(to, col), device_id_type=MESH,
        )

    def b_copy(c):
        to = jnp.where(role == 1, z + 1, z - 1)
        return pltpu.make_async_remote_copy(
            src_ref=pair.at[1, c], dst_ref=pair.at[2, c], send_sem=b_send.at[c], recv_sem=b_recv.at[c],
            device_id=(to, col), device_id_type=MESH,
        )

    def l_copy(c):
        to = jnp.where(role == 1, z - 1, lax.rem(z + 2, 8))
        return pltpu.make_async_remote_copy(
            src_ref=leads.at[2, c], dst_ref=leads.at[group, c], send_sem=l_send.at[c],
            recv_sem=l_recv.at[group, c], device_id=(to, col), device_id_type=MESH,
        )

    @pl.when(role != 1)
    def _():
        for c in range(CHUNKS):
            a_copy(c).start()

    def lower(first, last):
        @pl.loop(first, last)
        def _(q):
            rows = pl.ds(pl.multiple_of(q * 256, 256), 256)
            cbuf[rows, :] = cbuf[rows, :] - dot(vectors(q), wacc[...])
            pltpu.make_async_copy(cbuf.at[rows], out_hbm.at[rows], out_sem).start()

    chain = (role == 1) | (role == 2)
    cut = jnp.where(chain, jnp.int32(5), jnp.int32(CHIPS))

    pltpu.make_async_copy(fac_u.at[0], fac_u.at[0], sib2_sem).wait()

    def prepare(slot, foreign):
        at = jnp.where(foreign, jnp.int32(FOREIGN), jnp.int32(OWN_U))
        at = pl.multiple_of(at, 8)
        u = buf[:, pl.ds(at, 8), :].reshape(PANEL, PANEL)
        f = buf[:, pl.ds(at + 8, 8), :].reshape(PANEL, PANEL)
        fac_u[slot] = u
        fac_ut[slot] = u.T
        fac_ft[slot] = f.T

    prepare(0, (role == 2) | (z == 0))
    prepare(1, role == 1)

    lower(1, cut)

    def weights(slot, leader, partner):
        return dot(fac_ft[slot], leader + dot(fac_ut[slot], partner))

    @pl.when(role != 0)
    def _():
        for c in range(CHUNKS):
            a_copy(c).wait_recv()
            own, got = xown[c], pair[0, c]
            leader = jnp.where(role == 2, own, got)
            partner = jnp.where(role == 2, got, own)
            w = weights(0, leader, partner)
            pair[1, c] = leader - w

            @pl.when(chain)
            def _():
                b_copy(c).start()

            @pl.when(role != 2)
            def _():
                xfin[c] = partner - dot(fac_u[0], w)

    @pl.when(chain)
    def _():
        for c in range(CHUNKS):
            b_copy(c).wait_recv()
            own, got = pair[1, c], pair[2, c]
            leader = jnp.where(role == 1, own, got)
            partner = jnp.where(role == 1, got, own)
            w = weights(1, leader, partner)
            leads[2, c] = leader - w
            l_copy(c).start()

            @pl.when(role == 2)
            def _():
                xfin[c] = partner - dot(fac_u[1], w)

    lower(cut, CHIPS)

    @pl.when(role == 0)
    def _():
        for c in range(CHUNKS):
            for k in (0, 1):
                pltpu.make_async_copy(leads.at[k, c], leads.at[k, c], l_recv.at[k, c]).wait()
            leader, partner = leads[0, c], leads[1, c]
            w = weights(0, leader, partner)

            @pl.when(z == 0)
            def _():
                xfin[c] = leader - w

            @pl.when(z != 0)
            def _():
                xfin[c] = partner - dot(fac_u[0], w)

    tops = [
        pltpu.make_async_copy(xfin.at[c], out_hbm.at[pl.ds(0, PANEL), pl.ds(c * CHUNK, CHUNK)], top_sem.at[c])
        for c in range(CHUNKS)
    ]
    for t in tops:
        t.start()

    pltpu.make_async_copy(buf.at[pl.ds(0, DEVS - 1)], buf.at[pl.ds(0, DEVS - 1)], send_sem).wait()

    @pl.when(role != 1)
    def _():
        for c in range(CHUNKS):
            a_copy(c).wait_send()

    @pl.when(chain)
    def _():
        for c in range(CHUNKS):
            b_copy(c).wait_send()
            l_copy(c).wait_send()

    lower_rows = pl.ds(PANEL, ROWS - PANEL)
    pltpu.make_async_copy(cbuf.at[lower_rows], out_hbm.at[lower_rows], out_sem).wait()
    for t in tops:
        t.wait()


def shards(trailing, leaf_vectors, leaf_factor, tree_vectors, tree_factor):
    dma = pltpu.SemaphoreType.DMA
    return pl.pallas_call(
        kernel,
        out_shape=jax.ShapeDtypeStruct((ROWS, COLS), F32),
        in_specs=[pl.BlockSpec(memory_space=pl.ANY)] * 5,
        out_specs=pl.BlockSpec(memory_space=pl.ANY),
        scratch_shapes=[
            pltpu.VMEM((DEVS, BLOCK, PANEL), F32),
            pltpu.VMEM((ROWS, COLS), F32),
            pltpu.VMEM((PANEL, COLS), F32),
            pltpu.VMEM((PANEL, COLS), F32),
            pltpu.VMEM((CHUNKS, PANEL, CHUNK), F32),
            pltpu.VMEM((3, CHUNKS, PANEL, CHUNK), F32),
            pltpu.VMEM((3, CHUNKS, PANEL, CHUNK), F32),
            pltpu.VMEM((CHUNKS, PANEL, CHUNK), F32),
            pltpu.VMEM((2, PANEL, PANEL), F32),
            pltpu.VMEM((2, PANEL, PANEL), F32),
            pltpu.VMEM((2, PANEL, PANEL), F32),
            dma((5,)), dma, dma, dma((3, CHIPS)), dma((3, CHIPS)), dma((2, CHIPS)), dma, dma, dma,
            dma((CHUNKS,)), dma((CHUNKS,)), dma((CHUNKS,)), dma((CHUNKS,)), dma((CHUNKS,)), dma((2, CHUNKS)),
            dma, dma((CHUNKS,)),
        ],
        compiler_params=pltpu.CompilerParams(
            collective_id=0, has_side_effects=True, vmem_limit_bytes=50 * 1024 * 1024
        ),
    )(trailing, leaf_vectors, leaf_factor, tree_vectors, tree_factor)


def solution(mesh):
    placed = (
        P("row", "col"),
        P(("row", "col"), None),
        P(("row", "col"), None),
        P(("row", "col"), None),
        P(("row", "col"), None),
    )
    return jax.shard_map(
        shards, mesh=mesh, in_specs=placed, out_specs=P("row", "col"), check_vma=False
    )
```

time: 246 us -> 67.7 us (0.28)
  the two profiles are of different devices: /device:TPU:1 before, /device:TPU:4 now
where the time goes in v1:
time: 67.7 us; the launch traced here: 67.4 us
  Pallas kernels  58.5 us (86%)
  local copies, waits for them, and re-layouts  8.89 us (13%)
    pallas_call x1, Pallas kernels, shards(): pl.pallas_call(kernel, out_shape=jax.ShapeDtypeStruct((ROWS, COLS), F32),...  58.5 us
    unnamed x9, local copies, waits for them, and re-layouts  8.89 us

profile of v1, /device:TPU:4, one launch (start us, length us, event | category | flops | bytes accessed | tf_op | source)
XLA Modules:
  0.0 67.4 jit_solution(16674144507413551447)
XLA Ops:
  0.0 0.0 copy-start
  0.0 0.9 %copy-done = f32[128,256]{1,0:T(8,128)S(1)} copy-done((f32[128,256]{1,0:T(8,128)S(1)}, f32[128,256]{1,0:T(8,128)}, u32[]{:S(2)}) %copy-start) | copy-done | bytes 131096
  0.9 0.0 copy-start.1
  0.9 0.7 %copy-done.1 = f32[8,256]{1,0:T(8,128)S(1)} copy-done((f32[8,256]{1,0:T(8,128)S(1)}, f32[8,256]{1,0:T(8,128)}, u32[]{:S(2)}) %copy-start.1) | copy-done | bytes 8216
  1.6 0.0 copy-start.2
  1.6 0.7 %copy-done.2 = f32[8,256]{1,0:T(8,128)S(1)} copy-done((f32[8,256]{1,0:T(8,128)S(1)}, f32[8,256]{1,0:T(8,128)}, u32[]{:S(2)}) %copy-start.2) | copy-done | bytes 8216
  2.3 0.0 copy-start.3
  2.3 0.7 %copy-done.3 = f32[8,256]{1,0:T(8,128)S(1)} copy-done((f32[8,256]{1,0:T(8,128)S(1)}, f32[8,256]{1,0:T(8,128)}, u32[]{:S(2)}) %copy-start.3) | copy-done | bytes 8216
  3.0 58.5 %shard_map.55 = f32[4096,384]{1,0:T(8,128)} custom-call(f32[4096,384]{1,0:T(8,128)} %c_hbm.1, f32[128,256]{1,0:T(8,128)S(1)} %copy-done, f32[8,256]{1,0:T(8,128)S(1)} %copy-done.1, f32[8,256]{1,0:T(8,128)S(1)} %copy-done.2, f32[8,256]{1,0:T(8,128)S(1)} %copy-done.3), custom_call_target="tpu_custom_call" | custom-call | tf_op jit(solution)/shard_map/pallas_call | solution.py:320
  61.5 5.9 %copy.7 = f32[4096,384]{1,0:T(8,128)} copy(f32[4096,384]{1,0:T(8,128)} %shard_map.55) | data formatting | bytes 12582912
Async XLA Ops:
  0.0 0.9 %copy-start = (f32[128,256]{1,0:T(8,128)S(1)}, f32[128,256]{1,0:T(8,128)}, u32[]{:S(2)}) copy-start(f32[128,256]{1,0:T(8,128)} %v_hbm.1) | copy-start | bytes 393220
  0.9 0.7 %copy-start.1 = (f32[8,256]{1,0:T(8,128)S(1)}, f32[8,256]{1,0:T(8,128)}, u32[]{:S(2)}) copy-start(f32[8,256]{1,0:T(8,128)} %s_hbm.1) | copy-start | bytes 24580
  1.6 0.7 %copy-start.2 = (f32[8,256]{1,0:T(8,128)S(1)}, f32[8,256]{1,0:T(8,128)}, u32[]{:S(2)}) copy-start(f32[8,256]{1,0:T(8,128)} %u_hbm.1) | copy-start | bytes 24580
  2.3 0.7 %copy-start.3 = (f32[8,256]{1,0:T(8,128)S(1)}, f32[8,256]{1,0:T(8,128)}, u32[]{:S(2)}) copy-start(f32[8,256]{1,0:T(8,128)} %f_hbm.1) | copy-start | bytes 24580

commit v2 on v1

v2 whole, which is shorter than its diff:
```python
import jax
import jax.numpy as jnp
from jax import lax
from jax.experimental import pallas as pl
from jax.experimental.pallas import tpu as pltpu
from jax.sharding import PartitionSpec as P

MESH = pl.DeviceIdType.MESH
HIGH = lax.Precision.HIGH
F32 = jnp.float32

PANEL = 256
ROWS = 4096
COLS = 384
CHUNK = 64
CHUNKS = COLS // CHUNK
WIDE = 128
SIDE = 4
CHIPS = 16

BLOCK = 168
S_ROW, OWN, FOREIGN = 128, 136, 152
STREAMS = ((0, 64, 32, 0), (64, 72, 40, 1), (OWN, 32, 32, 1))


def pick(index, values):
    result = jnp.int32(values[-1])
    for k in range(len(values) - 2, -1, -1):
        result = jnp.where(index == k, jnp.int32(values[k]), result)
    return result


def product(a, b, dims):
    return lax.dot_general(a, b, (dims, ((), ())), precision=HIGH, preferred_element_type=F32)


def dot(a, b):
    return product(a, b, ((1,), (0,)))


def dot_t(a, b):
    return product(a, b, ((0,), (0,)))


def dot_nt(a, b):
    return product(a, b, ((1,), (1,)))


def kernel(
    c_hbm, v_hbm, s_hbm, u_hbm, f_hbm, cbuf,
    buf, zacc, wacc, xa, xb, leads, wt, xfin, fac_u, fac_w,
    load_sem, c_sem, send_sem, side_sem, recv_sem, half_sem, sib_sem, uf_send, uf_recv, tail_recv, tail_sib,
    a_send, a_recv, b_send, b_recv, l_send, l_recv,
):
    z = lax.axis_index("row")
    col = lax.axis_index("col")
    core = lax.rem(col, 2)
    chip = lax.div(col, 2)
    x = lax.div(chip, SIDE)
    y = lax.rem(chip, SIDE)
    role = lax.rem(z, 4)
    group = lax.div(z, 4)
    sibling = col + 1 - 2 * core

    def chip_at(dx, dy):
        return lax.rem(x + dx, SIDE) * SIDE + lax.rem(y + dy, SIDE)

    def neighbour(axis, step):
        return chip_at(step, 0) * 2 + core if axis == 0 else chip_at(0, step) * 2 + core

    own_block = buf.at[chip, core]
    loads = [
        pltpu.make_async_copy(v_hbm, own_block.at[pl.ds(0, 128)], load_sem.at[0]),
        pltpu.make_async_copy(s_hbm, own_block.at[pl.ds(S_ROW, 8)], load_sem.at[1]),
        pltpu.make_async_copy(u_hbm, own_block.at[pl.ds(OWN, 8)], load_sem.at[2]),
        pltpu.make_async_copy(f_hbm, own_block.at[pl.ds(OWN + 8, 8)], load_sem.at[3]),
    ]
    for load in loads:
        load.start()
    load_c = pltpu.make_async_copy(c_hbm, cbuf, c_sem)
    load_c.start()

    barrier = pltpu.get_barrier_semaphore()
    for axis in (0, 1):
        for step in (1, 2, 3):
            pl.semaphore_signal(barrier, inc=1, device_id=(z, neighbour(axis, step)), device_id_type=MESH)
    pl.semaphore_signal(barrier, inc=1, device_id=(z, sibling), device_id_type=MESH)
    for step in range(1, 8):
        pl.semaphore_signal(barrier, inc=1, device_id=(lax.rem(z + step, 8), col), device_id_type=MESH)
    pl.semaphore_wait(barrier, 14)
    for load in loads:
        load.wait()

    def send(place, start, rows, to, sem):
        pltpu.make_async_remote_copy(
            src_ref=buf.at[place, core, pl.ds(start, rows)], dst_ref=buf.at[place, core, pl.ds(start, rows)],
            send_sem=send_sem, recv_sem=sem, device_id=(z, to), device_id_type=MESH,
        ).start()

    def to_sibling(place, start, rows, sem):
        pltpu.make_async_remote_copy(
            src_ref=buf.at[place, core, pl.ds(start, rows)], dst_ref=buf.at[place, core, pl.ds(start, rows)],
            send_sem=side_sem, recv_sem=sem, device_id=(z, sibling), device_id_type=MESH,
        ).start()

    def arrived(place, half, start, rows, sem):
        ref = buf.at[place, half, pl.ds(start, rows)]
        pltpu.make_async_copy(ref, ref, sem).wait()

    def index(axis, i, j):
        i, j = i % SIDE, j % SIDE
        return (i * SIDE + j) if axis == 0 else (j * SIDE + i)

    def place_of(h, i, j):
        return chip_at(i, j) if STREAMS[h][3] == 0 else chip_at(j, i)

    def first_axis(h):
        start, rows, _, axis = STREAMS[h]
        for step in (1, 3, 2):
            send(chip, start, rows, neighbour(axis, step), recv_sem.at[h, index(axis, -step, 0)])

    def second_axis(h, i):
        start, rows, _, axis = STREAMS[h]
        place = place_of(h, i, 0)
        if h == 2:
            for step in (1, 3, 2):
                send(place, start, rows, neighbour(1 - axis, step), tail_recv)
        else:
            for step in (1, 3):
                send(place, start, rows, neighbour(1 - axis, step), recv_sem.at[h, index(axis, i, -step)])

    def handle(h, i, j):
        start, rows, front, axis = STREAMS[h]
        place = place_of(h, i, j)
        here = index(axis, i, j)
        if j == 2:
            arrived(place, core, start, front, recv_sem.at[h, here])
            arrived(place, core, start + front, rows - front, half_sem.at[h, here])
        else:
            arrived(place, core, start, rows, recv_sem.at[h, here])
        if j == 0:
            second_axis(h, i)
        elif j == 3:
            send(place, start, front, neighbour(1 - axis, 1), recv_sem.at[h, index(axis, i, 2)])
        elif j == 1:
            send(place, start + front, rows - front, neighbour(1 - axis, 3), half_sem.at[h, index(axis, i, 2)])
        if h < 2:
            to_sibling(place, start, rows, sib_sem.at[h, here])

    def both(*offsets):
        for i, j in offsets:
            for h in (0, 1):
                handle(h, i, j)

    def vectors(q):
        return buf[q, :, pl.ds(0, 128), :].reshape(PANEL, PANEL)

    def project(*chips):
        @pl.loop(0, len(chips))
        def _(t):
            dx = pick(t, [c[0] for c in chips])
            dy = pick(t, [c[1] for c in chips])
            q = chip_at(dx, dy)
            for h in (0, 1):
                arrived(q, 1 - core, STREAMS[h][0], STREAMS[h][1], sib_sem.at[h, dx * SIDE + dy])
            rows = pl.ds(pl.multiple_of(q * 256, 256), 256)
            zacc[...] += dot_t(vectors(q), cbuf[rows, :])

    first_axis(0)
    first_axis(1)
    second_axis(0, 0)
    second_axis(1, 0)
    uf_to = pick(z, (3, 4, 1, 2, 0, 7, 5, 6))
    uf_copy = pltpu.make_async_remote_copy(
        src_ref=buf.at[chip, core, pl.ds(OWN, 16)], dst_ref=buf.at[chip, core, pl.ds(FOREIGN, 16)],
        send_sem=uf_send, recv_sem=uf_recv, device_id=(uf_to, col), device_id_type=MESH,
    )
    uf_copy.start()
    for h in (0, 1):
        to_sibling(chip, STREAMS[h][0], STREAMS[h][1], sib_sem.at[h, 0])
    zacc[...] = jnp.zeros_like(zacc)
    load_c.wait()
    both((1, 0), (3, 0))
    both((2, 0))
    uf_copy.wait()
    first_axis(2)
    both((0, 1), (0, 3))
    project((0, 0), (1, 0), (3, 0), (0, 1), (0, 3))
    both((1, 1), (1, 3), (3, 1), (3, 3))
    both((0, 2))
    second_axis(2, 0)
    project((2, 0), (0, 2))
    both((2, 1), (2, 3))
    for i in (1, 3, 2):
        handle(2, i, 0)
    project((1, 1), (1, 3), (3, 1), (3, 3))
    both((1, 2), (3, 2))
    both((2, 2))
    project((1, 2), (3, 2), (2, 1), (2, 3), (2, 2))

    def rows_of(c):
        return pl.ds(pl.multiple_of(c * CHUNK, CHUNK), CHUNK)

    def a_copy(c):
        to = jnp.where(role == 3, z - 1, z + 1)
        return pltpu.make_async_remote_copy(
            src_ref=xa.at[0, rows_of(c)], dst_ref=xa.at[1, rows_of(c)], send_sem=a_send.at[c],
            recv_sem=a_recv.at[c], device_id=(to, col), device_id_type=MESH,
        )

    def b_copy(c):
        to = jnp.where(role == 1, z + 1, z - 1)
        return pltpu.make_async_remote_copy(
            src_ref=xb.at[0, rows_of(c)], dst_ref=xb.at[1, rows_of(c)], send_sem=b_send.at[c],
            recv_sem=b_recv.at[c], device_id=(to, col), device_id_type=MESH,
        )

    def l_copy(c):
        to = jnp.where(role == 1, z - 1, lax.rem(z + 2, 8))
        return pltpu.make_async_remote_copy(
            src_ref=leads.at[2, rows_of(c)], dst_ref=leads.at[group, rows_of(c)], send_sem=l_send.at[c],
            recv_sem=l_recv.at[group, c], device_id=(to, col), device_id_type=MESH,
        )

    factor = buf[:, :, pl.ds(S_ROW, 8), :].reshape(PANEL, PANEL)
    head = vectors(jnp.int32(0))
    for c in range(COLS // WIDE):
        wide = slice(c * WIDE, (c + 1) * WIDE)
        w = dot_t(factor, zacc[:, wide])
        wacc[:, wide] = w
        xa[0, pl.ds(c * WIDE, WIDE), :] = (cbuf[pl.ds(0, PANEL), wide] - dot(head, w)).T

        @pl.when(role != 1)
        def _():
            for k in range(c * WIDE // CHUNK, (c + 1) * WIDE // CHUNK):
                a_copy(k).start()

    def lower(first, last):
        @pl.loop(first, last)
        def _(q):
            rows = pl.ds(pl.multiple_of(q * 256, 256), 256)
            cbuf[rows, :] = cbuf[rows, :] - dot(vectors(q), wacc[...])

    chain = (role == 1) | (role == 2)
    cut = jnp.where(chain, jnp.int32(4), jnp.int32(CHIPS))

    pltpu.make_async_copy(xa.at[0], xa.at[0], tail_recv).wait()
    tail = pltpu.make_async_remote_copy(
        src_ref=buf.at[:, core, pl.ds(OWN, 32)], dst_ref=buf.at[:, core, pl.ds(OWN, 32)],
        send_sem=side_sem, recv_sem=tail_sib, device_id=(z, sibling), device_id_type=MESH,
    )
    tail.start()
    lower(1, cut)
    tail.wait_recv()

    def prepare(slot, foreign):
        at = pl.multiple_of(jnp.where(foreign, jnp.int32(FOREIGN), jnp.int32(OWN)), 8)
        u = buf[:, :, pl.ds(at, 8), :].reshape(PANEL, PANEL)
        f = buf[:, :, pl.ds(at + 8, 8), :].reshape(PANEL, PANEL)
        fac_u[slot] = u
        fac_w[slot, pl.ds(0, PANEL), :] = f
        fac_w[slot, pl.ds(PANEL, PANEL), :] = dot(u, f)

    prepare(0, (role == 2) | (z == 0))
    prepare(1, role == 1)

    def weights(slot, leader, partner):
        return dot(jnp.concatenate([leader, partner], axis=1), fac_w[slot])

    a_lead = jnp.where(role == 2, jnp.int32(0), jnp.int32(1))
    b_lead = jnp.where(role == 1, jnp.int32(0), jnp.int32(1))

    @pl.when(role != 0)
    def _():
        @pl.loop(0, CHUNKS)
        def _(c):
            a_copy(c).wait_recv()
            leader = xa[a_lead, rows_of(c), :]
            w = weights(0, leader, xa[1 - a_lead, rows_of(c), :])
            wt[0, rows_of(c), :] = w
            xb[0, rows_of(c), :] = leader - w

            @pl.when(chain)
            def _():
                b_copy(c).start()

    @pl.when(chain)
    def _():
        @pl.loop(0, CHUNKS)
        def _(c):
            b_copy(c).wait_recv()
            leader = xb[b_lead, rows_of(c), :]
            w = weights(1, leader, xb[1 - b_lead, rows_of(c), :])
            wt[1, rows_of(c), :] = w
            leads[2, rows_of(c), :] = leader - w
            l_copy(c).start()

    @pl.when((role == 1) | (role == 3))
    def _():
        xfin[...] = xa[0] - dot_nt(wt[0], fac_u[0])

    @pl.when(role == 2)
    def _():
        xfin[...] = xb[0] - dot_nt(wt[1], fac_u[1])

    lower(cut, CHIPS)

    @pl.when(role == 0)
    def _():
        @pl.loop(0, CHUNKS)
        def _(c):
            for k in (0, 1):
                ref = leads.at[k, rows_of(c)]
                pltpu.make_async_copy(ref, ref, l_recv.at[k, c]).wait()
            leader, partner = leads[0, rows_of(c), :], leads[1, rows_of(c), :]
            w = weights(0, leader, partner)

            @pl.when(z == 0)
            def _():
                xfin[rows_of(c), :] = leader - w

            @pl.when(z != 0)
            def _():
                xfin[rows_of(c), :] = partner - dot_nt(w, fac_u[0])

    for c in range(COLS // WIDE):
        cbuf[pl.ds(0, PANEL), c * WIDE : (c + 1) * WIDE] = xfin[pl.ds(c * WIDE, WIDE), :].T

    sent = buf.at[pl.ds(0, CHIPS - 1), 0]
    pltpu.make_async_copy(sent, sent, send_sem).wait()
    sent = buf.at[:, 0]
    pltpu.make_async_copy(sent, sent, side_sem).wait()

    @pl.when(role != 1)
    def _():
        for c in range(CHUNKS):
            a_copy(c).wait_send()

    @pl.when(chain)
    def _():
        for c in range(CHUNKS):
            b_copy(c).wait_send()
            l_copy(c).wait_send()


def shards(trailing, leaf_vectors, leaf_factor, tree_vectors, tree_factor):
    dma = pltpu.SemaphoreType.DMA
    return pl.pallas_call(
        kernel,
        out_shape=pltpu.VMEM((ROWS, COLS), F32),
        in_specs=[pl.BlockSpec(memory_space=pltpu.HBM)] * 5,
        out_specs=pl.BlockSpec(memory_space=pltpu.VMEM),
        scratch_shapes=[
            pltpu.VMEM((CHIPS, 2, BLOCK, PANEL), F32),
            pltpu.VMEM((PANEL, COLS), F32),
            pltpu.VMEM((PANEL, COLS), F32),
            pltpu.VMEM((2, COLS, PANEL), F32),
            pltpu.VMEM((2, COLS, PANEL), F32),
            pltpu.VMEM((3, COLS, PANEL), F32),
            pltpu.VMEM((2, COLS, PANEL), F32),
            pltpu.VMEM((COLS, PANEL), F32),
            pltpu.VMEM((2, PANEL, PANEL), F32),
            pltpu.VMEM((2, 2 * PANEL, PANEL), F32),
            dma((4,)), dma, dma, dma, dma((3, CHIPS)), dma((2, CHIPS)), dma((2, CHIPS)), dma, dma, dma, dma,
            dma((CHUNKS,)), dma((CHUNKS,)), dma((CHUNKS,)), dma((CHUNKS,)), dma((CHUNKS,)), dma((2, CHUNKS)),
        ],
        compiler_params=pltpu.CompilerParams(
            collective_id=0, has_side_effects=True, vmem_limit_bytes=44 * 1024 * 1024
        ),
    )(trailing, leaf_vectors, leaf_factor, tree_vectors, tree_factor)


def solution(mesh):
    placed = (
        P("row", "col"),
        P(("row", "col"), None),
        P(("row", "col"), None),
        P(("row", "col"), None),
        P(("row", "col"), None),
    )
    return jax.shard_map(
        shards, mesh=mesh, in_specs=placed, out_specs=P("row", "col"), check_vma=False
    )
```

time: 67.7 us -> 62.1 us (0.917)
  the two profiles are of different devices: /device:TPU:4 before, /device:TPU:1 now
where the time goes in v2:
time: 62.1 us; the launch traced here: 61.8 us
  Pallas kernels  56.1 us (90%)
  local copies, waits for them, and re-layouts  5.7 us (9%)
    pallas_call x1, Pallas kernels, shards(): pl.pallas_call(kernel, out_shape=pltpu.VMEM((ROWS, COLS), F32), in_specs=...  56.1 us
    unnamed x9, local copies, waits for them, and re-layouts  5.7 us

profile of v2, /device:TPU:1, one launch (start us, length us, event | category | flops | bytes accessed | tf_op | source)
XLA Modules:
  0.0 61.8 jit_solution(7239605886768093047)
XLA Ops:
  0.0 0.0 copy-start
  0.0 0.9 %copy-done = f32[128,256]{1,0:T(8,128)S(1)} copy-done((f32[128,256]{1,0:T(8,128)S(1)}, f32[128,256]{1,0:T(8,128)}, u32[]{:S(2)}) %copy-start) | copy-done | bytes 131096
  0.9 0.0 copy-start.1
  0.9 0.7 %copy-done.1 = f32[8,256]{1,0:T(8,128)S(1)} copy-done((f32[8,256]{1,0:T(8,128)S(1)}, f32[8,256]{1,0:T(8,128)}, u32[]{:S(2)}) %copy-start.1) | copy-done | bytes 8216
  1.6 0.0 copy-start.2
  1.6 0.7 %copy-done.2 = f32[8,256]{1,0:T(8,128)S(1)} copy-done((f32[8,256]{1,0:T(8,128)S(1)}, f32[8,256]{1,0:T(8,128)}, u32[]{:S(2)}) %copy-start.2) | copy-done | bytes 8216
  2.3 0.0 copy-start.3
  2.3 0.7 %copy-done.3 = f32[8,256]{1,0:T(8,128)S(1)} copy-done((f32[8,256]{1,0:T(8,128)S(1)}, f32[8,256]{1,0:T(8,128)}, u32[]{:S(2)}) %copy-start.3) | copy-done | bytes 8216
  3.0 56.1 %shard_map.55 = f32[4096,384]{1,0:T(8,128)S(1)} custom-call(f32[4096,384]{1,0:T(8,128)} %c_hbm.1, f32[128,256]{1,0:T(8,128)S(1)} %copy-done, f32[8,256]{1,0:T(8,128)S(1)} %copy-done.1, f32[8,256]{1,0:T(8,128)S(1)} %copy-done.2, f32[8,256]{1,0:T(8,128)S(1)} %copy-done.3), custom_call_target="tpu_custom_call" | custom-call | tf_op jit(solution)/shard_map/pallas_call | solution.py:348
  59.1 2.7 %copy.7 = f32[4096,384]{1,0:T(8,128)} copy(f32[4096,384]{1,0:T(8,128)S(1)} %shard_map.55) | data formatting | bytes 12582912
Async XLA Ops:
  0.0 0.9 %copy-start = (f32[128,256]{1,0:T(8,128)S(1)}, f32[128,256]{1,0:T(8,128)}, u32[]{:S(2)}) copy-start(f32[128,256]{1,0:T(8,128)} %v_hbm.1) | copy-start | bytes 393220
  0.9 0.7 %copy-start.1 = (f32[8,256]{1,0:T(8,128)S(1)}, f32[8,256]{1,0:T(8,128)}, u32[]{:S(2)}) copy-start(f32[8,256]{1,0:T(8,128)} %s_hbm.1) | copy-start | bytes 24580
  1.6 0.7 %copy-start.2 = (f32[8,256]{1,0:T(8,128)S(1)}, f32[8,256]{1,0:T(8,128)}, u32[]{:S(2)}) copy-start(f32[8,256]{1,0:T(8,128)} %u_hbm.1) | copy-start | bytes 24580
  2.3 0.7 %copy-start.3 = (f32[8,256]{1,0:T(8,128)S(1)}, f32[8,256]{1,0:T(8,128)}, u32[]{:S(2)}) copy-start(f32[8,256]{1,0:T(8,128)} %f_hbm.1) | copy-start | bytes 24580

commit v3 on v2

--- a/solution.py
+++ b/solution.py
@@ -8,6 +8,7 @@
 MESH = pl.DeviceIdType.MESH
 HIGH = lax.Precision.HIGH
 F32 = jnp.float32
+BF16 = jnp.bfloat16
 
 PANEL = 256
 ROWS = 4096
@@ -15,12 +16,13 @@
 CHUNK = 64
 CHUNKS = COLS // CHUNK
 WIDE = 128
+LAG = 3
 SIDE = 4
 CHIPS = 16
 
 BLOCK = 168
 S_ROW, OWN, FOREIGN = 128, 136, 152
-STREAMS = ((0, 64, 32, 0), (64, 72, 40, 1), (OWN, 32, 32, 1))
+STREAMS = ((0, 64, 32, 0), (64, 72, 40, 1), (OWN, 16, 16, 0), (FOREIGN, 16, 16, 1))
 
 
 def pick(index, values):
@@ -48,7 +50,7 @@
 
 def kernel(
     c_hbm, v_hbm, s_hbm, u_hbm, f_hbm, cbuf,
-    buf, zacc, wacc, xa, xb, leads, wt, xfin, fac_u, fac_w,
+    buf, zacc, wacc, xa, xb, leads, wt, xfin, fac_u, fac_high, fac_low,
     load_sem, c_sem, send_sem, side_sem, recv_sem, half_sem, sib_sem, uf_send, uf_recv, tail_recv, tail_sib,
     a_send, a_recv, b_send, b_recv, l_send, l_recv,
 ):
@@ -122,27 +124,27 @@
     def second_axis(h, i):
         start, rows, _, axis = STREAMS[h]
         place = place_of(h, i, 0)
-        if h == 2:
+        if h >= 2:
             for step in (1, 3, 2):
                 send(place, start, rows, neighbour(1 - axis, step), tail_recv)
         else:
-            for step in (1, 3):
+            for step in (1, 3, 2) if i == 2 else (1, 3):
                 send(place, start, rows, neighbour(1 - axis, step), recv_sem.at[h, index(axis, i, -step)])
 
     def handle(h, i, j):
         start, rows, front, axis = STREAMS[h]
         place = place_of(h, i, j)
         here = index(axis, i, j)
-        if j == 2:
+        if j == 2 and i != 2:
             arrived(place, core, start, front, recv_sem.at[h, here])
             arrived(place, core, start + front, rows - front, half_sem.at[h, here])
         else:
             arrived(place, core, start, rows, recv_sem.at[h, here])
         if j == 0:
             second_axis(h, i)
-        elif j == 3:
+        elif j == 3 and i != 2:
             send(place, start, front, neighbour(1 - axis, 1), recv_sem.at[h, index(axis, i, 2)])
-        elif j == 1:
+        elif j == 1 and i != 2:
             send(place, start + front, rows - front, neighbour(1 - axis, 3), half_sem.at[h, index(axis, i, 2)])
         if h < 2:
             to_sibling(place, start, rows, sib_sem.at[h, here])
@@ -182,17 +184,20 @@
     load_c.wait()
     both((1, 0), (3, 0))
     both((2, 0))
+    both((0, 1), (0, 3))
     uf_copy.wait()
     first_axis(2)
-    both((0, 1), (0, 3))
+    first_axis(3)
     project((0, 0), (1, 0), (3, 0), (0, 1), (0, 3))
     both((1, 1), (1, 3), (3, 1), (3, 3))
     both((0, 2))
-    second_axis(2, 0)
     project((2, 0), (0, 2))
     both((2, 1), (2, 3))
+    for h in (2, 3):
+        second_axis(h, 0)
     for i in (1, 3, 2):
         handle(2, i, 0)
+        handle(3, i, 0)
     project((1, 1), (1, 3), (3, 1), (3, 3))
     both((1, 2), (3, 2))
     both((2, 2))
@@ -253,47 +258,85 @@
     lower(1, cut)
     tail.wait_recv()
 
-    def prepare(slot, foreign):
+    def store_factor(slot, start, value):
+        high = value.astype(BF16)
+        fac_high[slot, pl.ds(start, PANEL), :] = high
+        fac_low[slot, pl.ds(start, PANEL), :] = (value - high.astype(F32)).astype(BF16)
+
+    def prepare(slot, foreign, last):
         at = pl.multiple_of(jnp.where(foreign, jnp.int32(FOREIGN), jnp.int32(OWN)), 8)
         u = buf[:, :, pl.ds(at, 8), :].reshape(PANEL, PANEL)
         f = buf[:, :, pl.ds(at + 8, 8), :].reshape(PANEL, PANEL)
         fac_u[slot] = u
-        fac_w[slot, pl.ds(0, PANEL), :] = f
-        fac_w[slot, pl.ds(PANEL, PANEL), :] = dot(u, f)
-
-    prepare(0, (role == 2) | (z == 0))
-    prepare(1, role == 1)
+        uf = dot(u, f)
+        if last is None:
+            store_factor(slot, 0, f)
+            store_factor(slot, PANEL, uf)
+        else:
+
+            @pl.when(jnp.logical_not(last))
+            def _():
+                store_factor(slot, 0, f)
+                store_factor(slot, PANEL, uf)
+
+            @pl.when(last)
+            def _():
+                store_factor(slot, 0, dot_nt(f, u))
+                store_factor(slot, PANEL, dot_nt(uf, u))
+
+    prepare(0, (role == 2) | (z == 0), z == 4)
+
+    @pl.when(chain)
+    def _():
+        prepare(1, role == 1, None)
+
+    def plain(a, b):
+        return jnp.dot(a, b, preferred_element_type=F32)
 
     def weights(slot, leader, partner):
-        return dot(jnp.concatenate([leader, partner], axis=1), fac_w[slot])
+        count = leader.shape[0]
+        both_rows = jnp.concatenate([leader, partner], axis=1)
+        high = both_rows.astype(BF16)
+        low = (both_rows - high.astype(F32)).astype(BF16)
+        main = plain(jnp.concatenate([high, low], axis=0), fac_high[slot])
+        return main[:count] + (main[count:] + plain(high, fac_low[slot]))
 
     a_lead = jnp.where(role == 2, jnp.int32(0), jnp.int32(1))
     b_lead = jnp.where(role == 1, jnp.int32(0), jnp.int32(1))
 
-    @pl.when(role != 0)
+    def a_step(c):
+        a_copy(c).wait_recv()
+        leader = xa[a_lead, rows_of(c), :]
+        w = weights(0, leader, xa[1 - a_lead, rows_of(c), :])
+        wt[0, rows_of(c), :] = w
+        return leader - w
+
+    def b_step(c):
+        b_copy(c).wait_recv()
+        leader = xb[b_lead, rows_of(c), :]
+        w = weights(1, leader, xb[1 - b_lead, rows_of(c), :])
+        leads[2, rows_of(c), :] = leader - w
+        l_copy(c).start()
+        wt[1, rows_of(c), :] = w
+
+    @pl.when(role == 3)
     def _():
         @pl.loop(0, CHUNKS)
         def _(c):
-            a_copy(c).wait_recv()
-            leader = xa[a_lead, rows_of(c), :]
-            w = weights(0, leader, xa[1 - a_lead, rows_of(c), :])
-            wt[0, rows_of(c), :] = w
-            xb[0, rows_of(c), :] = leader - w
-
-            @pl.when(chain)
+            a_step(c)
+
+    @pl.when(chain)
+    def _():
+        @pl.loop(0, CHUNKS + LAG)
+        def _(t):
+            @pl.when(t < CHUNKS)
             def _():
-                b_copy(c).start()
-
-    @pl.when(chain)
-    def _():
-        @pl.loop(0, CHUNKS)
-        def _(c):
-            b_copy(c).wait_recv()
-            leader = xb[b_lead, rows_of(c), :]
-            w = weights(1, leader, xb[1 - b_lead, rows_of(c), :])
-            wt[1, rows_of(c), :] = w
-            leads[2, rows_of(c), :] = leader - w
-            l_copy(c).start()
+                xb[0, rows_of(t), :] = a_step(t)
+                b_copy(t).start()
+
+            @pl.when(t >= LAG)
+            def _():
+                b_step(t - LAG)
 
     @pl.when((role == 1) | (role == 3))
     def _():
@@ -301,30 +344,29 @@
 
     @pl.when(role == 2)
     def _():
-        xfin[...] = xb[0] - dot_nt(wt[1], fac_u[1])
+        xfin[...] = xb[1 - b_lead] - dot_nt(wt[1], fac_u[1])
 
     lower(cut, CHIPS)
 
+    def store_top(c, value):
+        cbuf[pl.ds(0, PANEL), pl.ds(pl.multiple_of(c * WIDE, WIDE), WIDE)] = value.T
+
+    @pl.when(role != 0)
+    def _():
+        for c in range(COLS // WIDE):
+            store_top(c, xfin[pl.ds(c * WIDE, WIDE), :])
+
     @pl.when(role == 0)
     def _():
-        @pl.loop(0, CHUNKS)
+        @pl.loop(0, COLS // WIDE)
         def _(c):
             for k in (0, 1):
-                ref = leads.at[k, rows_of(c)]
-                pltpu.make_async_copy(ref, ref, l_recv.at[k, c]).wait()
-            leader, partner = leads[0, rows_of(c), :], leads[1, rows_of(c), :]
-            w = weights(0, leader, partner)
-
-            @pl.when(z == 0)
-            def _():
-                xfin[rows_of(c), :] = leader - w
-
-            @pl.when(z != 0)
-            def _():
-                xfin[rows_of(c), :] = partner - dot_nt(w, fac_u[0])
-
-    for c in range(COLS // WIDE):
-        cbuf[pl.ds(0, PANEL), c * WIDE : (c + 1) * WIDE] = xfin[pl.ds(c * WIDE, WIDE), :].T
+                for half in range(WIDE // CHUNK):
+                    ref = leads.at[k, pl.ds(0, CHUNK)]
+                    pltpu.make_async_copy(ref, ref, l_recv.at[k, c * (WIDE // CHUNK) + half]).wait()
+            rows = pl.ds(pl.multiple_of(c * WIDE, WIDE), WIDE)
+            w = weights(0, leads[0, rows, :], leads[1, rows, :])
+            store_top(c, leads[group, rows, :] - w)
 
     sent = buf.at[pl.ds(0, CHIPS - 1), 0]
     pltpu.make_async_copy(sent, sent, send_sem).wait()
@@ -360,12 +402,13 @@
             pltpu.VMEM((2, COLS, PANEL), F32),
             pltpu.VMEM((COLS, PANEL), F32),
             pltpu.VMEM((2, PANEL, PANEL), F32),
-            pltpu.VMEM((2, 2 * PANEL, PANEL), F32),
-            dma((4,)), dma, dma, dma, dma((3, CHIPS)), dma((2, CHIPS)), dma((2, CHIPS)), dma, dma, dma, dma,
+            pltpu.VMEM((2, 2 * PANEL, PANEL), BF16),
+            pltpu.VMEM((2, 2 * PANEL, PANEL), BF16),
+            dma((4,)), dma, dma, dma, dma((4, CHIPS)), dma((2, CHIPS)), dma((2, CHIPS)), dma, dma, dma, dma,
             dma((CHUNKS,)), dma((CHUNKS,)), dma((CHUNKS,)), dma((CHUNKS,)), dma((CHUNKS,)), dma((2, CHUNKS)),
         ],
         compiler_params=pltpu.CompilerParams(
-            collective_id=0, has_side_effects=True, vmem_limit_bytes=44 * 1024 * 1024
+            collective_id=0, has_side_effects=True, vmem_limit_bytes=57 * 1024 * 1024
         ),
     )(trailing, leaf_vectors, leaf_factor, tree_vectors, tree_factor)
 

time: 62.1 us -> 55 us (0.89)
  Pallas kernels: 56.1 us -> 51.6 us
  local copies, waits for them, and re-layouts: 5.7 us -> 2.71 us
    pallas_call x1, Pallas kernels: 56.1 us -> 51.6 us  [shards(): pl.pallas_call(kernel, out_shape=pltpu.VMEM((ROWS, COLS), F32), in_specs=...]
    unnamed x9 -> x1, local copies, waits for them, and re-layouts: 5.7 us -> 2.71 us
where the time goes in v3:
time: 55 us; the launch traced here: 54.3 us
  Pallas kernels  51.6 us (94%)
  local copies, waits for them, and re-layouts  2.71 us (5%)
    pallas_call x1, Pallas kernels, shards(): pl.pallas_call(kernel, out_shape=pltpu.VMEM((ROWS, COLS), F32), in_specs=...  51.6 us
    unnamed x1, local copies, waits for them, and re-layouts  2.71 us

profile of v3, /device:TPU:1, one launch (start us, length us, event | category | flops | bytes accessed | tf_op | source)
XLA Modules:
  0.0 54.3 jit_solution(3493424613563509072)
XLA Ops:
  0.0 51.6 %shard_map.55 = f32[4096,384]{1,0:T(8,128)S(1)} custom-call(f32[4096,384]{1,0:T(8,128)} %c_hbm.1, f32[128,256]{1,0:T(8,128)} %v_hbm.1, f32[8,256]{1,0:T(8,128)} %s_hbm.1, f32[8,256]{1,0:T(8,128)} %u_hbm.1, f32[8,256]{1,0:T(8,128)} %f_hbm.1), custom_call_target="tpu_custom_call" | custom-call | tf_op jit(solution)/shard_map/pallas_call | solution.py:390
  51.6 2.7 %copy.7 = f32[4096,384]{1,0:T(8,128)} copy(f32[4096,384]{1,0:T(8,128)S(1)} %shard_map.55) | data formatting | bytes 12582912

commit v4 on v3

--- a/solution.py
+++ b/solution.py
@@ -17,6 +17,7 @@
 CHUNKS = COLS // CHUNK
 WIDE = 128
 LAG = 3
+GROUP = 128
 SIDE = 4
 CHIPS = 16
 
@@ -48,9 +49,25 @@
     return product(a, b, ((1,), (1,)))
 
 
+def plain(a, b):
+    return jnp.dot(a, b, preferred_element_type=F32)
+
+
+def halves(value):
+    high = value.astype(BF16)
+    return high, (value - high.astype(F32)).astype(BF16)
+
+
+def split_dot(a, b_high, b_low):
+    count = a.shape[0]
+    high, low = halves(a)
+    main = plain(jnp.concatenate([high, low], axis=0), b_high)
+    return main[:count] + (main[count:] + plain(high, b_low))
+
+
 def kernel(
     c_hbm, v_hbm, s_hbm, u_hbm, f_hbm, cbuf,
-    buf, zacc, wacc, xa, xb, leads, wt, xfin, fac_u, fac_high, fac_low,
+    buf, zt, ct, w_high, w_low, xa, xb, leads, wt, xfin, fac_u, fac_high, fac_low,
     load_sem, c_sem, send_sem, side_sem, recv_sem, half_sem, sib_sem, uf_send, uf_recv, tail_recv, tail_sib,
     a_send, a_recv, b_send, b_recv, l_send, l_recv,
 ):
@@ -128,23 +145,23 @@
             for step in (1, 3, 2):
                 send(place, start, rows, neighbour(1 - axis, step), tail_recv)
         else:
-            for step in (1, 3, 2) if i == 2 else (1, 3):
+            for step in (1, 3):
                 send(place, start, rows, neighbour(1 - axis, step), recv_sem.at[h, index(axis, i, -step)])
 
     def handle(h, i, j):
         start, rows, front, axis = STREAMS[h]
         place = place_of(h, i, j)
         here = index(axis, i, j)
-        if j == 2 and i != 2:
+        if j == 2:
             arrived(place, core, start, front, recv_sem.at[h, here])
             arrived(place, core, start + front, rows - front, half_sem.at[h, here])
         else:
             arrived(place, core, start, rows, recv_sem.at[h, here])
         if j == 0:
             second_axis(h, i)
-        elif j == 3 and i != 2:
+        elif j == 3:
             send(place, start, front, neighbour(1 - axis, 1), recv_sem.at[h, index(axis, i, 2)])
-        elif j == 1 and i != 2:
+        elif j == 1:
             send(place, start + front, rows - front, neighbour(1 - axis, 3), half_sem.at[h, index(axis, i, 2)])
         if h < 2:
             to_sibling(place, start, rows, sib_sem.at[h, here])
@@ -166,7 +183,7 @@
             for h in (0, 1):
                 arrived(q, 1 - core, STREAMS[h][0], STREAMS[h][1], sib_sem.at[h, dx * SIDE + dy])
             rows = pl.ds(pl.multiple_of(q * 256, 256), 256)
-            zacc[...] += dot_t(vectors(q), cbuf[rows, :])
+            zt[...] += dot_t(cbuf[rows, :], vectors(q))
 
     first_axis(0)
     first_axis(1)
@@ -180,8 +197,9 @@
     uf_copy.start()
     for h in (0, 1):
         to_sibling(chip, STREAMS[h][0], STREAMS[h][1], sib_sem.at[h, 0])
-    zacc[...] = jnp.zeros_like(zacc)
+    zt[...] = jnp.zeros_like(zt)
     load_c.wait()
+    ct[...] = cbuf[pl.ds(0, PANEL), :].T
     both((1, 0), (3, 0))
     both((2, 0))
     both((0, 1), (0, 3))
@@ -200,8 +218,9 @@
         handle(3, i, 0)
     project((1, 1), (1, 3), (3, 1), (3, 3))
     both((1, 2), (3, 2))
+    project((1, 2), (3, 2), (2, 1), (2, 3))
     both((2, 2))
-    project((1, 2), (3, 2), (2, 1), (2, 3), (2, 2))
+    project((2, 2))
 
     def rows_of(c):
         return pl.ds(pl.multiple_of(c * CHUNK, CHUNK), CHUNK)
@@ -227,27 +246,29 @@
             recv_sem=l_recv.at[group, c], device_id=(to, col), device_id_type=MESH,
         )
 
-    factor = buf[:, :, pl.ds(S_ROW, 8), :].reshape(PANEL, PANEL)
-    head = vectors(jnp.int32(0))
-    for c in range(COLS // WIDE):
-        wide = slice(c * WIDE, (c + 1) * WIDE)
-        w = dot_t(factor, zacc[:, wide])
-        wacc[:, wide] = w
-        xa[0, pl.ds(c * WIDE, WIDE), :] = (cbuf[pl.ds(0, PANEL), wide] - dot(head, w)).T
+    s_halves = halves(buf[:, :, pl.ds(S_ROW, 8), :].reshape(PANEL, PANEL))
+    head_halves = halves(vectors(jnp.int32(0)).T)
+    for g in range(COLS // GROUP):
+        rows = pl.ds(g * GROUP, GROUP)
+        w = split_dot(zt[rows, :], *s_halves)
+        zt[rows, :] = w
+        xa[0, rows, :] = ct[rows, :] - split_dot(w, *head_halves)
 
         @pl.when(role != 1)
         def _():
-            for k in range(c * WIDE // CHUNK, (c + 1) * WIDE // CHUNK):
+            for k in range(g * GROUP // CHUNK, (g + 1) * GROUP // CHUNK):
                 a_copy(k).start()
+
+    w_high[...], w_low[...] = halves(zt[...].T)
 
     def lower(first, last):
         @pl.loop(first, last)
         def _(q):
             rows = pl.ds(pl.multiple_of(q * 256, 256), 256)
-            cbuf[rows, :] = cbuf[rows, :] - dot(vectors(q), wacc[...])
+            cbuf[rows, :] = cbuf[rows, :] - split_dot(vectors(q), w_high[...], w_low[...])
 
     chain = (role == 1) | (role == 2)
-    cut = jnp.where(chain, jnp.int32(4), jnp.int32(CHIPS))
+    cut = jnp.where(chain, jnp.int32(9), jnp.int32(CHIPS))
 
     pltpu.make_async_copy(xa.at[0], xa.at[0], tail_recv).wait()
     tail = pltpu.make_async_remote_copy(
@@ -259,9 +280,8 @@
     tail.wait_recv()
 
     def store_factor(slot, start, value):
-        high = value.astype(BF16)
-        fac_high[slot, pl.ds(start, PANEL), :] = high
-        fac_low[slot, pl.ds(start, PANEL), :] = (value - high.astype(F32)).astype(BF16)
+        rows = pl.ds(start, PANEL)
+        fac_high[slot, rows, :], fac_low[slot, rows, :] = halves(value)
 
     def prepare(slot, foreign, last):
         at = pl.multiple_of(jnp.where(foreign, jnp.int32(FOREIGN), jnp.int32(OWN)), 8)
@@ -290,16 +310,8 @@
     def _():
         prepare(1, role == 1, None)
 
-    def plain(a, b):
-        return jnp.dot(a, b, preferred_element_type=F32)
-
     def weights(slot, leader, partner):
-        count = leader.shape[0]
-        both_rows = jnp.concatenate([leader, partner], axis=1)
-        high = both_rows.astype(BF16)
-        low = (both_rows - high.astype(F32)).astype(BF16)
-        main = plain(jnp.concatenate([high, low], axis=0), fac_high[slot])
-        return main[:count] + (main[count:] + plain(high, fac_low[slot]))
+        return split_dot(jnp.concatenate([leader, partner], axis=1), fac_high[slot], fac_low[slot])
 
     a_lead = jnp.where(role == 2, jnp.int32(0), jnp.int32(1))
     b_lead = jnp.where(role == 1, jnp.int32(0), jnp.int32(1))
@@ -358,15 +370,16 @@
 
     @pl.when(role == 0)
     def _():
-        @pl.loop(0, COLS // WIDE)
-        def _(c):
+        done = 0
+        for c in range(CHUNKS):
             for k in (0, 1):
-                for half in range(WIDE // CHUNK):
-                    ref = leads.at[k, pl.ds(0, CHUNK)]
-                    pltpu.make_async_copy(ref, ref, l_recv.at[k, c * (WIDE // CHUNK) + half]).wait()
-            rows = pl.ds(pl.multiple_of(c * WIDE, WIDE), WIDE)
-            w = weights(0, leads[0, rows, :], leads[1, rows, :])
-            store_top(c, leads[group, rows, :] - w)
+                ref = leads.at[k, rows_of(c)]
+                pltpu.make_async_copy(ref, ref, l_recv.at[k, c]).wait()
+            w = weights(0, leads[0, rows_of(c), :], leads[1, rows_of(c), :])
+            xfin[rows_of(c), :] = leads[group, rows_of(c), :] - w
+            while (done + 1) * WIDE <= (c + 1) * CHUNK:
+                store_top(done, xfin[pl.ds(done * WIDE, WIDE), :])
+                done += 1
 
     sent = buf.at[pl.ds(0, CHIPS - 1), 0]
     pltpu.make_async_copy(sent, sent, send_sem).wait()
@@ -394,8 +407,10 @@
         out_specs=pl.BlockSpec(memory_space=pltpu.VMEM),
         scratch_shapes=[
             pltpu.VMEM((CHIPS, 2, BLOCK, PANEL), F32),
-            pltpu.VMEM((PANEL, COLS), F32),
-            pltpu.VMEM((PANEL, COLS), F32),
+            pltpu.VMEM((COLS, PANEL), F32),
+            pltpu.VMEM((COLS, PANEL), F32),
+            pltpu.VMEM((PANEL, COLS), BF16),
+            pltpu.VMEM((PANEL, COLS), BF16),
             pltpu.VMEM((2, COLS, PANEL), F32),
             pltpu.VMEM((2, COLS, PANEL), F32),
             pltpu.VMEM((3, COLS, PANEL), F32),

time: 55 us -> 53.7 us (0.976)
  Pallas kernels: 51.6 us -> 50.2 us
    pallas_call x1, Pallas kernels: 51.6 us -> 50.2 us  [shards(): pl.pallas_call(kernel, out_shape=pltpu.VMEM((ROWS, COLS), F32), in_specs=...]
where the time goes in v4:
time: 53.7 us; the launch traced here: 52.9 us
  Pallas kernels  50.2 us (93%)
  local copies, waits for them, and re-layouts  2.71 us (5%)
    pallas_call x1, Pallas kernels, shards(): pl.pallas_call(kernel, out_shape=pltpu.VMEM((ROWS, COLS), F32), in_specs=...  50.2 us
    unnamed x1, local copies, waits for them, and re-layouts  2.71 us

profile of v4, /device:TPU:1, one launch (start us, length us, event | category | flops | bytes accessed | tf_op | source)
XLA Modules:
  0.0 52.9 jit_solution(9419897154640858069)
XLA Ops:
  0.0 50.2 %shard_map.55 = f32[4096,384]{1,0:T(8,128)S(1)} custom-call(f32[4096,384]{1,0:T(8,128)} %c_hbm.1, f32[128,256]{1,0:T(8,128)} %v_hbm.1, f32[8,256]{1,0:T(8,128)} %s_hbm.1, f32[8,256]{1,0:T(8,128)} %u_hbm.1, f32[8,256]{1,0:T(8,128)} %f_hbm.1), custom_call_target="tpu_custom_call" | custom-call | tf_op jit(solution)/shard_map/pallas_call | solution.py:403
  50.2 2.7 %copy.7 = f32[4096,384]{1,0:T(8,128)} copy(f32[4096,384]{1,0:T(8,128)S(1)} %shard_map.55) | data formatting | bytes 12582912

commit v5 on v4

--- a/solution.py
+++ b/solution.py
@@ -17,7 +17,7 @@
 CHUNKS = COLS // CHUNK
 WIDE = 128
 LAG = 3
-GROUP = 128
+GROUP = 64
 SIDE = 4
 CHIPS = 16
 
@@ -259,8 +259,6 @@
             for k in range(g * GROUP // CHUNK, (g + 1) * GROUP // CHUNK):
                 a_copy(k).start()
 
-    w_high[...], w_low[...] = halves(zt[...].T)
-
     def lower(first, last):
         @pl.loop(first, last)
         def _(q):
@@ -268,7 +266,7 @@
             cbuf[rows, :] = cbuf[rows, :] - split_dot(vectors(q), w_high[...], w_low[...])
 
     chain = (role == 1) | (role == 2)
-    cut = jnp.where(chain, jnp.int32(9), jnp.int32(CHIPS))
+    cut = jnp.where(chain, jnp.int32(5), jnp.int32(CHIPS))
 
     pltpu.make_async_copy(xa.at[0], xa.at[0], tail_recv).wait()
     tail = pltpu.make_async_remote_copy(
@@ -276,6 +274,7 @@
         send_sem=side_sem, recv_sem=tail_sib, device_id=(z, sibling), device_id_type=MESH,
     )
     tail.start()
+    w_high[...], w_low[...] = halves(zt[...].T)
     lower(1, cut)
     tail.wait_recv()
 
@@ -306,10 +305,6 @@
 
     prepare(0, (role == 2) | (z == 0), z == 4)
 
-    @pl.when(chain)
-    def _():
-        prepare(1, role == 1, None)
-
     def weights(slot, leader, partner):
         return split_dot(jnp.concatenate([leader, partner], axis=1), fac_high[slot], fac_low[slot])
 
@@ -339,16 +334,23 @@
 
     @pl.when(chain)
     def _():
-        @pl.loop(0, CHUNKS + LAG)
+        def forward(t):
+            xb[0, rows_of(t), :] = a_step(t)
+            b_copy(t).start()
+
+        @pl.loop(0, LAG)
+        def _(t):
+            forward(t)
+
+        prepare(1, role == 1, None)
+
+        @pl.loop(LAG, CHUNKS + LAG)
         def _(t):
             @pl.when(t < CHUNKS)
             def _():
-                xb[0, rows_of(t), :] = a_step(t)
-                b_copy(t).start()
-
-            @pl.when(t >= LAG)
-            def _():
-                b_step(t - LAG)
+                forward(t)
+
+            b_step(t - LAG)
 
     @pl.when((role == 1) | (role == 3))
     def _():

time: 53.7 us -> 53.8 us (level); the launches traced: 52.9 us -> 53.7 us
  Pallas kernels: 50.2 us -> 51 us
    pallas_call x1, Pallas kernels: 50.2 us -> 51 us  [shards(): pl.pallas_call(kernel, out_shape=pltpu.VMEM((ROWS, COLS), F32), in_specs=...]
where the time goes in v5:
time: 53.8 us; the launch traced here: 53.7 us
  Pallas kernels  51 us (95%)
  local copies, waits for them, and re-layouts  2.71 us (5%)
    pallas_call x1, Pallas kernels, shards(): pl.pallas_call(kernel, out_shape=pltpu.VMEM((ROWS, COLS), F32), in_specs=...  51 us
    unnamed x1, local copies, waits for them, and re-layouts  2.71 us

profile of v5, /device:TPU:1, one launch (start us, length us, event | category | flops | bytes accessed | tf_op | source)
XLA Modules:
  0.0 53.7 jit_solution(5892365271411814925)
XLA Ops:
  0.0 51.0 %shard_map.55 = f32[4096,384]{1,0:T(8,128)S(1)} custom-call(f32[4096,384]{1,0:T(8,128)} %c_hbm.1, f32[128,256]{1,0:T(8,128)} %v_hbm.1, f32[8,256]{1,0:T(8,128)} %s_hbm.1, f32[8,256]{1,0:T(8,128)} %u_hbm.1, f32[8,256]{1,0:T(8,128)} %f_hbm.1), custom_call_target="tpu_custom_call" | custom-call | tf_op jit(solution)/shard_map/pallas_call | solution.py:405
  51.0 2.7 %copy.7 = f32[4096,384]{1,0:T(8,128)} copy(f32[4096,384]{1,0:T(8,128)S(1)} %shard_map.55) | data formatting | bytes 12582912

commit v6 on v5

--- a/solution.py
+++ b/solution.py
@@ -135,7 +135,7 @@
 
     def first_axis(h):
         start, rows, _, axis = STREAMS[h]
-        for step in (1, 3, 2):
+        for step in (1, 3) if h < 2 else (1, 3, 2):
             send(chip, start, rows, neighbour(axis, step), recv_sem.at[h, index(axis, -step, 0)])
 
     def second_axis(h, i):
@@ -152,12 +152,16 @@
         start, rows, front, axis = STREAMS[h]
         place = place_of(h, i, j)
         here = index(axis, i, j)
-        if j == 2:
+        if j == 2 or (h < 2 and j == 0 and i == 2):
             arrived(place, core, start, front, recv_sem.at[h, here])
             arrived(place, core, start + front, rows - front, half_sem.at[h, here])
         else:
             arrived(place, core, start, rows, recv_sem.at[h, here])
         if j == 0:
+            if h < 2 and i == 3:
+                send(place, start, front, neighbour(axis, 1), recv_sem.at[h, index(axis, 2, 0)])
+            if h < 2 and i == 1:
+                send(place, start + front, rows - front, neighbour(axis, 3), half_sem.at[h, index(axis, 2, 0)])
             second_axis(h, i)
         elif j == 3:
             send(place, start, front, neighbour(1 - axis, 1), recv_sem.at[h, index(axis, i, 2)])
@@ -201,8 +205,8 @@
     load_c.wait()
     ct[...] = cbuf[pl.ds(0, PANEL), :].T
     both((1, 0), (3, 0))
+    both((0, 1), (0, 3))
     both((2, 0))
-    both((0, 1), (0, 3))
     uf_copy.wait()
     first_axis(2)
     first_axis(3)

time: 53.8 us -> 54.4 us (1.011)
  Pallas kernels: 51 us -> 51.6 us
    pallas_call x1, Pallas kernels: 51 us -> 51.6 us  [shards(): pl.pallas_call(kernel, out_shape=pltpu.VMEM((ROWS, COLS), F32), in_specs=...]
where the time goes in v6:
time: 54.4 us; the launch traced here: 54.3 us
  Pallas kernels  51.6 us (95%)
  local copies, waits for them, and re-layouts  2.71 us (5%)
    pallas_call x1, Pallas kernels, shards(): pl.pallas_call(kernel, out_shape=pltpu.VMEM((ROWS, COLS), F32), in_specs=...  51.6 us
    unnamed x1, local copies, waits for them, and re-layouts  2.71 us

profile of v6, /device:TPU:1, one launch (start us, length us, event | category | flops | bytes accessed | tf_op | source)
XLA Modules:
  0.0 54.3 jit_solution(3824846400601821018)
XLA Ops:
  0.0 51.6 %shard_map.55 = f32[4096,384]{1,0:T(8,128)S(1)} custom-call(f32[4096,384]{1,0:T(8,128)} %c_hbm.1, f32[128,256]{1,0:T(8,128)} %v_hbm.1, f32[8,256]{1,0:T(8,128)} %s_hbm.1, f32[8,256]{1,0:T(8,128)} %u_hbm.1, f32[8,256]{1,0:T(8,128)} %f_hbm.1), custom_call_target="tpu_custom_call" | custom-call | tf_op jit(solution)/shard_map/pallas_call | solution.py:409
  51.6 2.7 %copy.7 = f32[4096,384]{1,0:T(8,128)} copy(f32[4096,384]{1,0:T(8,128)S(1)} %shard_map.55) | data formatting | bytes 12582912
